TPU v7x, 32 devices: a whole 2x2x4 slice. The times are simulated.
32 devices in a mesh: dp: 2 (over y), ctx: 8 (over z, x), tensor: 2 (over core).
Axes of the slice: x: 2, y: 2, z: 4, core: 2. Of those that a mesh axis runs over, the one named last changes fastest.
Arguments:
- queries: bfloat16 [2048, 8192], P(('dp', 'ctx'), 'tensor'), parts along dimension 0, may hold values from -6 to 6
- keys: bfloat16 [2048, 1024], P(('dp', 'ctx'), 'tensor'), parts along dimension 0, may hold values from -6 to 6
- values: bfloat16 [2048, 1024], P(('dp', 'ctx'), 'tensor'), parts along dimension 0, may hold values from -6 to 6
- attn_out: bfloat16 [2048, 8192], P(('dp', 'ctx'), 'tensor'), parts along dimension 0, may hold values from -6 to 6
- grad_out: bfloat16 [2048, 8192], P(('dp', 'ctx'), 'tensor'), parts along dimension 0, may hold values from -6 to 6
- log_norm: float32 [64, 2048], P('tensor', ('dp', 'ctx')), parts along dimension 1, may hold values from 3 to 6
- doc_lengths: int32 [32], P('dp'), parts along dimension 0, may hold values from 1 to 256, 1024 in all
- block_order: int32 [32], P('dp'), parts along dimension 0, may hold values from 0 to 15, each once
Outputs:
- grad_queries: bfloat16 [2048, 8192], P(('dp', 'ctx'), 'tensor'), parts along dimension 0
- key_gradient_rows: bfloat16 [2048, 1024], P(('dp', 'ctx'), 'tensor'), parts along dimension 0
- value_gradient_rows: bfloat16 [2048, 1024], P(('dp', 'ctx'), 'tensor'), parts along dimension 0
There are 2 independent parts, one for each index of `dp`. A program takes and returns all parts, laid end to end along the dimension named above; each array names one. Nothing has to cross between parts.
Inputs may be any that keep to these rules, and one draw needn't show every extreme that they name: `doc_lengths`: document lengths in sequence order; they sum to 1024 and the largest is exactly 256. `block_order`: each of the 16 blocks of 64 positions appears once.
All inputs are finite; a program needn't handle non-finite values.
Results may differ from a plain program's by a relative error of at most 0.0049.
Values may be sent and summed in bfloat16 or wider, within the bound.
A program may use at most 64 MiB of HBM per device.

v0:
```python
import math

import jax
import jax.numpy as jnp
from jax import lax
from jax.sharding import PartitionSpec as P

QUERY_HEADS = 64
KEY_VALUE_HEADS = 8
HEAD_SIZE = 128


def from_behind(block, axis, distance):
    devices = range(lax.axis_size(axis))
    route = [((i - distance) % len(devices), i) for i in devices]
    return lax.ppermute(block, axis, route)


def on_device(queries, keys, values, attn_out, grad_out, log_norm, doc_lengths, block_order):
    row_count, row_width = queries.shape
    kv_width = keys.shape[1]
    local_kv = kv_width // HEAD_SIZE
    query_group_width = QUERY_HEADS // KEY_VALUE_HEADS
    cycle_size = lax.axis_size("ctx")
    my_index = lax.axis_index("ctx")
    half_rows = row_count // 2
    doc_ends = jnp.cumsum(doc_lengths)
    local_rows = jnp.arange(row_count, dtype=jnp.int32)
    score_scale = 1.0 / math.sqrt(HEAD_SIZE)

    def positions(source):
        pair_blocks = lax.dynamic_slice_in_dim(block_order, source * 2, 2)
        starts = jnp.repeat(pair_blocks, half_rows, total_repeat_length=row_count) * half_rows
        position = starts + local_rows % half_rows
        doc_ids = jnp.sum((position[:, None] >= doc_ends[None, :]).astype(jnp.int32), axis=1)
        return (position, doc_ids)

    query_pos, query_doc = positions(my_index)
    query_heads = queries.reshape(row_count, local_kv, query_group_width, HEAD_SIZE)
    grad_heads = grad_out.reshape(row_count, local_kv, query_group_width, HEAD_SIZE)
    out_heads = attn_out.reshape(row_count, local_kv, query_group_width, HEAD_SIZE)
    out_dot = jnp.einsum(
        "rkgd,rkgd->kgr", grad_heads, out_heads, preferred_element_type=jnp.float32
    )
    log_norms = log_norm.reshape(local_kv, query_group_width, row_count)

    def full_terms(key_value, allowed):
        key_block = key_value[0].reshape(row_count, local_kv, HEAD_SIZE)
        value_block = key_value[1].reshape(row_count, local_kv, HEAD_SIZE)
        scores = (
            jnp.einsum("rkgd,ckd->kgrc", query_heads, key_block, preferred_element_type=jnp.float32)
            * score_scale
        )
        weights = jnp.where(allowed[None, None], jnp.exp(scores - log_norms[..., None]), 0.0)
        grad_weights = jnp.einsum(
            "rkgd,ckd->kgrc", grad_heads, value_block, preferred_element_type=jnp.float32
        )
        grad_scores = (weights * (grad_weights - out_dot[..., None]) * score_scale).astype(
            jnp.bfloat16
        )
        weights_bf = weights.astype(jnp.bfloat16)
        grad_query = jnp.einsum(
            "kgrc,ckd->rkgd", grad_scores, key_block, preferred_element_type=jnp.float32
        )
        grad_key = jnp.einsum(
            "kgrc,rkgd->ckd", grad_scores, query_heads, preferred_element_type=jnp.float32
        )
        grad_value = jnp.einsum(
            "kgrc,rkgd->ckd", weights_bf, grad_heads, preferred_element_type=jnp.float32
        )
        grad_pair = jnp.stack(
            [grad_key.reshape(row_count, kv_width), grad_value.reshape(row_count, kv_width)]
        )
        return (grad_query.reshape(row_count, row_width), grad_pair)

    def contribute(key_value, source):
        key_pos, key_doc = positions(source)
        allowed = (query_doc[:, None] == key_doc[None, :]) & (
            key_pos[None, :] <= query_pos[:, None]
        )
        return full_terms(key_value, allowed)

    initial = jnp.zeros((cycle_size, 2, row_count, kv_width), jnp.float32)

    def absorb(stored, partial_value, source):
        return lax.dynamic_update_index_in_dim(stored, partial_value, source, 0)

    def one_turn(step_index, loop_state):
        key_value, stored, grad_q = loop_state
        source = (my_index - step_index) % cycle_size
        part_q, partial_value = contribute(key_value, source)
        stored = absorb(stored, partial_value, source)
        key_value = from_behind(key_value, "ctx", 1)
        return (key_value, stored, grad_q + part_q)

    start_state = (
        jnp.stack([keys, values]),
        initial,
        jnp.zeros((row_count, row_width), jnp.float32),
    )
    key_value, stored, grad_q = lax.fori_loop(0, cycle_size - 1, one_turn, start_state)
    last_source = (my_index + 1) % cycle_size
    part_q, partial_value = contribute(key_value, last_source)
    stored = absorb(stored, partial_value, last_source)
    grad_q = grad_q + part_q
    received = lax.all_to_all(stored, "ctx", split_axis=0, concat_axis=0, tiled=True)
    summed = jnp.sum(received, axis=0)
    return (
        grad_q.astype(jnp.bfloat16),
        summed[0].astype(jnp.bfloat16),
        summed[1].astype(jnp.bfloat16),
    )


def solution(mesh):
    placed = (
        P(("dp", "ctx"), "tensor"),
        P(("dp", "ctx"), "tensor"),
        P(("dp", "ctx"), "tensor"),
        P(("dp", "ctx"), "tensor"),
        P(("dp", "ctx"), "tensor"),
        P("tensor", ("dp", "ctx")),
        P("dp"),
        P("dp"),
    )
    return jax.shard_map(
        on_device,
        mesh=mesh,
        in_specs=placed,
        out_specs=(
            P(("dp", "ctx"), "tensor"),
            P(("dp", "ctx"), "tensor"),
            P(("dp", "ctx"), "tensor"),
        ),
        check_vma=False,
    )
```

profile of v0, /device:TPU:0, one launch (start us, length us, event | category | flops | bytes accessed | tf_op | source)
XLA Modules:
  0.0 195.9 jit_solution(13182522378395927908)
XLA Ops:
  2.2 1.0 copy.79
  3.2 1.7 copy.80
  4.9 1.6 copy.83
  7.2 1.4 copy.131
  8.6 1.9 copy.110
  10.5 2.3 %multiply_reduce_fusion = f32[4,8,128]{1,0,2:T(4,128)S(1)} fusion(f32[4,8,128,128]{3,1,0,2:T(8,128)} %copy.110, bf16[128,4,8,128]{3,2,1,0:T(8,128)(2,1)S(1)} %bitcast.185), kind=kLoop, calls=%fused_computation.27 | loop fusion | flops 1568768 | bytes 3162112
  14.3 3.1 %fusion.22 = (s32[128]{0:T(128)S(1)}, s32[128]{0:T(128)S(1)}) fusion(pred[128]{0:T(512)(128)(4,1)} %constant.378, s32[]{:T(128)} %bitcast.5, s32[]{:T(128)} %bitcast.4, s32[]{:T(128)} %bitcast.15, s32[]{:T(128)} %bitcast.14), kind=kLoop, calls=%fused_computation.43 | loop fusion | flops 1536 | bytes 1168 | tf_op jit(solution)/shard_map/add | solution.py:34
  18.2 0.9 pad_maximum_fusion
  19.2 2.4 %broadcast_in_dim.110 = f32[8,2,128,512]{2,3,1,0:T(8,128)} broadcast(f32[]{:T(128)} %constant.347.clone.1), dimensions={} | broadcast | bytes 4194308 | tf_op jit(solution)/shard_map/broadcast_in_dim | solution.py:83
  21.6 71.3 %while.25 = (s32[]{:T(128)}, bf16[2,128,512]{1,2,0:T(8,128)(2,1)S(1)}, f32[8,2,128,512]{2,3,1,0:T(8,128)}, f32[128,4096]{0,1:T(8,128)}, s32[128]{0:T(128)S(1)}, ...) while((s32[]{:T(128)}, ...), condition=%wide.region_4.7_spmd.clone, body=%wide.region_2.0_spmd.clone.sunk | while | flops 676518912 | bytes 42930388 | solution.py:101
  21.7 3.0 %collective-permute-start = (bf16[2,128,512]{1,2,0:T(8,128)(2,1)S(1)}, bf16[2,128,512]{1,2,0:T(8,128)(2,1)S(1)}, u32[]{:S(2)}, u32[]{:S(2)}) collective-permute-start(bf16[2,128,512]{1,2,0:T(8,128)(2,1)S(1)} %copy.138), channel_id=1, source_target_pairs={{14,0},{0,2},{2,4},{4,6},{6,8},{8,10},{10,12},{12,14},{15,1},{1,3}... | collective-permute-start | bytes 786440 | tf_op jit(solution)/shard_map/while/body/eval_jaxpr/ppermute | solution.py:16
  25.4 1.2 fusion.82
  28.8 1.2 copy-done
  30.4 1.4 copy-done.1
  33.0 1.0 collective-permute-done
  35.4 1.2 fusion.82
  38.8 1.2 copy-done
  40.4 1.4 copy-done.1
  42.2 0.9 fusion.87
  43.1 1.2 collective-permute-done
  45.3 1.2 fusion.82
  48.8 1.2 copy-done
  50.3 1.4 copy-done.1
  53.6 1.0 collective-permute-start
  55.4 1.2 fusion.82
  58.8 1.2 copy-done
  60.4 1.4 copy-done.1
  62.2 0.9 fusion.87
  63.1 1.5 collective-permute-start
  65.3 1.2 fusion.82
  68.7 1.2 copy-done
  70.3 1.4 copy-done.1
  73.0 1.7 collective-permute-start
  75.4 1.2 fusion.82
  78.8 1.2 copy-done
  80.4 1.4 copy-done.1
  83.1 1.4 collective-permute-start
  85.2 1.2 fusion.82
  88.6 1.2 copy-done
  90.2 1.4 copy-done.1
  94.9 0.9 fusion.20
  95.8 4.8 %all-to-all-start = ((f32[8,2,128,512]{2,3,1,0:T(8,128)}), f32[8,2,128,512]{2,3,1,0:T(8,128)}, u32[]{:S(2)}, u32[]{:S(2)}) async-start(f32[8,2,128,512]{2,3,1,0:T(8,128)} %fusion.20), calls=%async_computation | async-start | bytes 8388608 | tf_op jit(solution)/shard_map/all_to_all | solution.py:106
  100.6 1.9 copy.89
  102.5 1.8 fusion.31
  104.2 3.0 %copy.90 = f32[128,4096]{1,0:T(8,128)} copy(f32[128,4096]{0,1:T(8,128)} %bitcast.184) | data formatting | bytes 4194304 | tf_op jit(solution)/shard_map/reshape | solution.py:74
  107.3 2.8 %add_convert_fusion = bf16[128,4096]{1,0:T(8,128)(2,1)} fusion(f32[128,4096]{1,0:T(8,128)S(1)} %copy-done.3, f32[128,4096]{1,0:T(8,128)} %copy.90), kind=kLoop, calls=%fused_computation.28 | loop fusion | flops 1048576 | bytes 5242880 | tf_op jit(solution)/shard_map/convert_element_type | solution.py:109
  110.1 81.9 %all-to-all-done = f32[8,2,128,512]{2,3,1,0:T(8,128)} async-done(((f32[8,2,128,512]{2,3,1,0:T(8,128)}), f32[8,2,128,512]{2,3,1,0:T(8,128)}, u32[]{:S(2)}, u32[]{:S(2)}) %all-to-all-start) | async-done | bytes 4194336 | tf_op jit(solution)/shard_map/all_to_all | solution.py:106
  192.0 2.4 %reduce_sum.47 = bf16[2,128,512]{1,2,0:T(8,128)(2,1)S(1)} reduce(f32[8,2,128,512]{2,3,1,0:T(8,128)} %all-to-all-done, f32[]{:T(128)} %constant.347.clone.1), dimensions={0}, to_apply=%region_6.9 | reduce | flops 917504 | bytes 4456452 | tf_op jit(solution)/shard_map/reduce_sum | solution.py:107
  (142 shorter events, 40.0 us)
Async XLA Ops:
  0.6 5.9 %copy-start.4 = (bf16[128,4096]{1,0:T(8,128)(2,1)S(1)}, bf16[128,4096]{1,0:T(8,128)(2,1)}, u32[]{:S(2)}) copy-start(bf16[128,4096]{1,0:T(8,128)(2,1)} %param.20) | copy-start | bytes 3145732
  19.2 2.5 %copy-start.5 = (f32[32,128]{1,0:T(8,128)S(1)}, f32[32,128]{1,0:T(8,128)}, u32[]{:S(2)}) copy-start(f32[32,128]{1,0:T(8,128)} %param.25) | copy-start | bytes 49156
  19.2 2.4 %copy-start.6 = (pred[128]{0:T(512)(128)(4,1)S(1)}, pred[128]{0:T(512)(128)(4,1)}, u32[]{:S(2)}) copy-start(pred[128]{0:T(512)(128)(4,1)} %constant.378) | copy-start | bytes 388
  19.2 2.4 %copy-start.7 = (s32[16]{0:T(128)S(1)}, s32[16]{0:T(128)}, u32[]{:S(2)}) copy-start(s32[16]{0:T(128)} %param.27) | copy-start | bytes 196
  19.2 2.4 %copy-start.8 = (s32[16]{0:T(128)S(1)}, s32[16]{0:T(128)}, u32[]{:S(2)}) copy-start(s32[16]{0:T(128)} %reduce.8) | copy-start | bytes 196
  21.7 12.3 %collective-permute-start = (bf16[2,128,512]{1,2,0:T(8,128)(2,1)S(1)}, bf16[2,128,512]{1,2,0:T(8,128)(2,1)S(1)}, u32[]{:S(2)}, u32[]{:S(2)}) collective-permute-start(bf16[2,128,512]{1,2,0:T(8,128)(2,1)S(1)} %copy.138), channel_id=1, source_target_pairs={{14,0},{0,2},{2,4},{4,6},{6,8},{8,10},{10,12},{12,14},{15,1},{1,3}... | collective-permute-start | bytes 786440 | tf_op jit(solution)/shard_map/while/body/eval_jaxpr/ppermute | solution.py:16
  28.4 1.6 copy-start
  30.4 1.4 copy-start.1
  34.0 10.2 %collective-permute-start = (bf16[2,128,512]{1,2,0:T(8,128)(2,1)S(1)}, bf16[2,128,512]{1,2,0:T(8,128)(2,1)S(1)}, u32[]{:S(2)}, u32[]{:S(2)}) collective-permute-start(bf16[2,128,512]{1,2,0:T(8,128)(2,1)S(1)} %copy.138), channel_id=1, source_target_pairs={{14,0},{0,2},{2,4},{4,6},{6,8},{8,10},{10,12},{12,14},{15,1},{1,3}... | collective-permute-start | bytes 786440 | tf_op jit(solution)/shard_map/while/body/eval_jaxpr/ppermute | solution.py:16
  38.4 1.6 copy-start
  40.4 1.4 copy-start.1
  44.3 9.3 %collective-permute-start = (bf16[2,128,512]{1,2,0:T(8,128)(2,1)S(1)}, bf16[2,128,512]{1,2,0:T(8,128)(2,1)S(1)}, u32[]{:S(2)}, u32[]{:S(2)}) collective-permute-start(bf16[2,128,512]{1,2,0:T(8,128)(2,1)S(1)} %copy.138), channel_id=1, source_target_pairs={{14,0},{0,2},{2,4},{4,6},{6,8},{8,10},{10,12},{12,14},{15,1},{1,3}... | collective-permute-start | bytes 786440 | tf_op jit(solution)/shard_map/while/body/eval_jaxpr/ppermute | solution.py:16
  48.3 1.6 copy-start
  50.3 1.4 copy-start.1
  53.6 9.4 %collective-permute-start = (bf16[2,128,512]{1,2,0:T(8,128)(2,1)S(1)}, bf16[2,128,512]{1,2,0:T(8,128)(2,1)S(1)}, u32[]{:S(2)}, u32[]{:S(2)}) collective-permute-start(bf16[2,128,512]{1,2,0:T(8,128)(2,1)S(1)} %copy.138), channel_id=1, source_target_pairs={{14,0},{0,2},{2,4},{4,6},{6,8},{8,10},{10,12},{12,14},{15,1},{1,3}... | collective-permute-start | bytes 786440 | tf_op jit(solution)/shard_map/while/body/eval_jaxpr/ppermute | solution.py:16
  58.4 1.6 copy-start
  60.4 1.4 copy-start.1
  63.1 9.9 %collective-permute-start = (bf16[2,128,512]{1,2,0:T(8,128)(2,1)S(1)}, bf16[2,128,512]{1,2,0:T(8,128)(2,1)S(1)}, u32[]{:S(2)}, u32[]{:S(2)}) collective-permute-start(bf16[2,128,512]{1,2,0:T(8,128)(2,1)S(1)} %copy.138), channel_id=1, source_target_pairs={{14,0},{0,2},{2,4},{4,6},{6,8},{8,10},{10,12},{12,14},{15,1},{1,3}... | collective-permute-start | bytes 786440 | tf_op jit(solution)/shard_map/while/body/eval_jaxpr/ppermute | solution.py:16
  68.3 1.6 copy-start
  70.3 1.4 copy-start.1
  73.0 10.1 %collective-permute-start = (bf16[2,128,512]{1,2,0:T(8,128)(2,1)S(1)}, bf16[2,128,512]{1,2,0:T(8,128)(2,1)S(1)}, u32[]{:S(2)}, u32[]{:S(2)}) collective-permute-start(bf16[2,128,512]{1,2,0:T(8,128)(2,1)S(1)} %copy.138), channel_id=1, source_target_pairs={{14,0},{0,2},{2,4},{4,6},{6,8},{8,10},{10,12},{12,14},{15,1},{1,3}... | collective-permute-start | bytes 786440 | tf_op jit(solution)/shard_map/while/body/eval_jaxpr/ppermute | solution.py:16
  78.4 1.6 copy-start
  80.4 1.4 copy-start.1
  83.1 9.8 %collective-permute-start = (bf16[2,128,512]{1,2,0:T(8,128)(2,1)S(1)}, bf16[2,128,512]{1,2,0:T(8,128)(2,1)S(1)}, u32[]{:S(2)}, u32[]{:S(2)}) collective-permute-start(bf16[2,128,512]{1,2,0:T(8,128)(2,1)S(1)} %copy.138), channel_id=1, source_target_pairs={{14,0},{0,2},{2,4},{4,6},{6,8},{8,10},{10,12},{12,14},{15,1},{1,3}... | collective-permute-start | bytes 786440 | tf_op jit(solution)/shard_map/while/body/eval_jaxpr/ppermute | solution.py:16
  88.2 1.6 copy-start
  90.2 1.4 copy-start.1
  95.8 4.8 %copy-start.2 = (f32[128,4096]{0,1:T(8,128)S(1)}, f32[128,4096]{0,1:T(8,128)}, u32[]{:S(2)}) copy-start(f32[128,4096]{0,1:T(8,128)} %get-tuple-element.501) | copy-start | bytes 6291460
  95.8 96.2 %all-to-all-start = ((f32[8,2,128,512]{2,3,1,0:T(8,128)}), f32[8,2,128,512]{2,3,1,0:T(8,128)}, u32[]{:S(2)}, u32[]{:S(2)}) async-start(f32[8,2,128,512]{2,3,1,0:T(8,128)} %fusion.20), calls=%async_computation | async-start | bytes 8388608 | tf_op jit(solution)/shard_map/all_to_all | solution.py:106
  104.2 3.1 %copy-start.3 = (f32[128,4096]{1,0:T(8,128)S(1)}, f32[128,4096]{1,0:T(8,128)}, u32[]{:S(2)}) copy-start(f32[128,4096]{1,0:T(8,128)} %copy.89) | copy-start | bytes 6291460
where the time goes:
time: 197 us; the launch traced here: 196 us
  waiting for transfers between devices  84.7 us (43%)
  local copies, waits for them, and re-layouts  42.2 us (21%)
  other arithmetic  32.4 us (16%)
  matrix products  20.7 us (11%)
  starting transfers between devices  14.4 us (7%)
    all_to_all x1, waiting for transfers between devices, on_device(): lax.all_to_all(stored, 'ctx', split_axis=0, concat_axis=0, tiled=True)  81.9 us
    while x35, local copies, waits for them, and re-layouts  17.9 us
    add x8, other arithmetic, positions(): position = starts + local_rows % half_rows  11.6 us
    unnamed x22, local copies, waits for them, and re-layouts  9.84 us
    ppermute x7, starting transfers between devices, from_behind(): return lax.ppermute(block, axis, route)  9.6 us
    dynamic_update_slice x8, other arithmetic, absorb(): return lax.dynamic_update_index_in_dim(stored, partial_value, source, 0)  6.74 us
    dot_general x8, matrix products, full_terms(): jnp.einsum('rkgd,ckd->kgrc', query_heads, key_block, preferred_element_ty...  4.8 us
    all_to_all x1, starting transfers between devices, on_device(): lax.all_to_all(stored, 'ctx', split_axis=0, concat_axis=0, tiled=True)  4.78 us
  transfers between devices with their start and end apart: 8, of which 4 were waited for; matrix products, arithmetic and copies ran while one was open for 25% of the time, Pallas kernels for 0%

commit v1 on v0

v1 whole, which is shorter than its diff:
```python
import functools
import math

import jax
import jax.numpy as jnp
from jax import lax
from jax.experimental import pallas as pl
from jax.experimental.pallas import tpu as pltpu
from jax.sharding import PartitionSpec as P

QUERY_HEADS = 64
KEY_VALUE_HEADS = 8
HEAD_SIZE = 128
GROUP = QUERY_HEADS // KEY_VALUE_HEADS
BLOCK = 64
MESH = pl.DeviceIdType.MESH
VMEM_LIMIT = 48 * 1024 * 1024
F32 = jnp.float32
BF16 = jnp.bfloat16


def neighbours(n, visit):
    me = lax.axis_index("ctx")
    row = me // 2
    visit(None, me + 1 - 2 * (me % 2))
    visit(row > 0, me - 2)
    visit(row < n // 2 - 1, me + 2)


def enter(n):
    barrier = pltpu.get_barrier_semaphore()

    def greet(condition, device):
        def signal():
            pl.semaphore_signal(barrier, inc=1, device_id={"ctx": device}, device_id_type=MESH)

        if condition is None:
            signal()
        else:
            pl.when(condition)(signal)

    neighbours(n, greet)
    row = lax.axis_index("ctx") // 2
    ends = (row > 0).astype(jnp.int32) + (row < n // 2 - 1).astype(jnp.int32)
    pl.semaphore_wait(barrier, 1 + ends)


def gather_kernel(n, k_ref, v_ref, all_ref, line_sem, pair_sem, recv_sem):
    lines = n // 2
    me = lax.axis_index("ctx")
    row, col = me // 2, me % 2
    partner = me + 1 - 2 * col
    sources = (k_ref, v_ref)
    enter(n)

    def remote(src, slot, half, sem, device):
        return pltpu.make_async_remote_copy(
            src_ref=src,
            dst_ref=all_ref.at[slot, half],
            send_sem=sem,
            recv_sem=recv_sem.at[slot, half],
            device_id={"ctx": device},
            device_id_type=MESH,
        )

    for half in range(2):
        @pl.when(row > 0)
        def _():
            remote(sources[half], me, half, line_sem.at[0, me, half], me - 2).start()

        @pl.when(row < lines - 1)
        def _():
            remote(sources[half], me, half, line_sem.at[1, me, half], me + 2).start()

        remote(sources[half], me, half, pair_sem.at[me, half], partner).start()
    for half in range(2):
        all_ref[me, half] = sources[half][...]

    def arrived(slot, half):
        remote(all_ref.at[slot, half], slot, half, pair_sem.at[slot, half], partner).wait_recv()

    for step in range(1, lines):
        for half in range(2):
            @pl.when(row - step >= 0)
            def _():
                slot = me - 2 * step
                arrived(slot, half)

                @pl.when(row < lines - 1)
                def _():
                    remote(
                        all_ref.at[slot, half], slot, half, line_sem.at[1, slot, half], me + 2
                    ).start()

                remote(
                    all_ref.at[slot, half], slot, half, pair_sem.at[slot, half], partner
                ).start()

            @pl.when(row + step < lines)
            def _():
                slot = me + 2 * step
                arrived(slot, half)

                @pl.when(row > 0)
                def _():
                    remote(
                        all_ref.at[slot, half], slot, half, line_sem.at[0, slot, half], me - 2
                    ).start()

                remote(
                    all_ref.at[slot, half], slot, half, pair_sem.at[slot, half], partner
                ).start()

    for line in range(lines):
        for half in range(2):
            arrived(2 * line + 1 - col, half)
    for line in range(lines):
        slot = 2 * line + col
        for half in range(2):
            remote(
                all_ref.at[slot, half], slot, half, pair_sem.at[slot, half], partner
            ).wait_send()

            @pl.when((line >= row) & (row > 0))
            def _():
                remote(
                    all_ref.at[slot, half], slot, half, line_sem.at[0, slot, half], me - 2
                ).wait_send()

            @pl.when((line <= row) & (row < lines - 1))
            def _():
                remote(
                    all_ref.at[slot, half], slot, half, line_sem.at[1, slot, half], me + 2
                ).wait_send()


def gather(n, keys, values):
    rows, width = keys.shape
    return pl.pallas_call(
        functools.partial(gather_kernel, n),
        out_shape=jax.ShapeDtypeStruct((n, 2, rows, width), BF16),
        in_specs=[pl.BlockSpec(memory_space=pltpu.VMEM)] * 2,
        out_specs=pl.BlockSpec(memory_space=pltpu.VMEM),
        scratch_shapes=[
            pltpu.SemaphoreType.DMA((2, n, 2)),
            pltpu.SemaphoreType.DMA((n, 2)),
            pltpu.SemaphoreType.DMA((n, 2)),
        ],
        compiler_params=pltpu.CompilerParams(
            collective_id=0, has_side_effects=True, vmem_limit_bytes=VMEM_LIMIT
        ),
        name="gather_kv",
    )(keys, values)


def reduce_kernel(
    n, part_ref, dk_ref, dv_ref, pair_buf, down_buf, up_buf, stage,
    pair_send, pair_recv, line_send, down_recv, up_recv,
):
    lines = n // 2
    me = lax.axis_index("ctx")
    row, col = me // 2, me % 2
    partner = me + 1 - 2 * col
    outs = (dk_ref, dv_ref)
    enter(n)

    def to_partner(line, half):
        return pltpu.make_async_remote_copy(
            src_ref=part_ref.at[2 * line + 1 - col, half],
            dst_ref=pair_buf.at[line, half],
            send_sem=pair_send.at[line, half],
            recv_sem=pair_recv.at[line, half],
            device_id={"ctx": partner},
            device_id_type=MESH,
        )

    def along(line, half, buf, recv, device):
        return pltpu.make_async_remote_copy(
            src_ref=stage.at[line, half],
            dst_ref=buf.at[line, half],
            send_sem=line_send.at[line, half],
            recv_sem=recv.at[line, half],
            device_id={"ctx": device},
            device_id_type=MESH,
        )

    def farthest_first(visit):
        for step in range(lines - 1, 0, -1):
            for half in range(2):
                @pl.when(row - step >= 0)
                def _():
                    visit(row - step, half, -1)

                @pl.when(row + step < lines)
                def _():
                    visit(row + step, half, 1)

    farthest_first(lambda line, half, way: to_partner(line, half).start())
    for half in range(2):
        to_partner(row, half).start()

    def pair_sum(line, half):
        to_partner(line, half).wait_recv()
        own = part_ref[2 * line + col, half].astype(F32)
        return own + pair_buf[line, half].astype(F32)

    def pass_on(line, half, way):
        total = pair_sum(line, half)
        if way < 0:
            stage[line, half] = total.astype(BF16)

            @pl.when(row < lines - 1)
            def _():
                along(line, half, down_buf, down_recv, me - 2).wait_recv()
                stage[line, half] = (total + down_buf[line, half].astype(F32)).astype(BF16)

            along(line, half, down_buf, down_recv, me - 2).start()
        else:
            stage[line, half] = total.astype(BF16)

            @pl.when(row > 0)
            def _():
                along(line, half, up_buf, up_recv, me + 2).wait_recv()
                stage[line, half] = (total + up_buf[line, half].astype(F32)).astype(BF16)

            along(line, half, up_buf, up_recv, me + 2).start()

    farthest_first(pass_on)

    for half in range(2):
        @pl.when(row == 0)
        def _():
            total = pair_sum(row, half)
            along(row, half, down_buf, down_recv, me + 2).wait_recv()
            outs[half][...] = (total + down_buf[row, half].astype(F32)).astype(BF16)

        @pl.when(row == lines - 1)
        def _():
            total = pair_sum(row, half)
            along(row, half, up_buf, up_recv, me - 2).wait_recv()
            outs[half][...] = (total + up_buf[row, half].astype(F32)).astype(BF16)

        @pl.when((row > 0) & (row < lines - 1))
        def _():
            total = pair_sum(row, half)
            along(row, half, down_buf, down_recv, me + 2).wait_recv()
            along(row, half, up_buf, up_recv, me - 2).wait_recv()
            outs[half][...] = (
                total + down_buf[row, half].astype(F32) + up_buf[row, half].astype(F32)
            ).astype(BF16)

    for line in range(lines):
        for half in range(2):
            to_partner(line, half).wait_send()

            @pl.when(row != line)
            def _():
                along(line, half, down_buf, down_recv, partner).wait_send()


def reduce_to_owner(n, parts):
    rows, width = parts.shape[2:]
    lines = n // 2
    buf = pltpu.VMEM((lines, 2, rows, width), BF16)
    sems = pltpu.SemaphoreType.DMA((lines, 2))
    return pl.pallas_call(
        functools.partial(reduce_kernel, n),
        out_shape=[jax.ShapeDtypeStruct((rows, width), BF16)] * 2,
        in_specs=[pl.BlockSpec(memory_space=pltpu.VMEM)],
        out_specs=[pl.BlockSpec(memory_space=pltpu.VMEM)] * 2,
        scratch_shapes=[buf] * 4 + [sems] * 5,
        compiler_params=pltpu.CompilerParams(
            collective_id=1, has_side_effects=True, vmem_limit_bytes=VMEM_LIMIT
        ),
        name="reduce_kv_grads",
    )(parts)


def terms_kernel(
    window, order_ref, lengths_ref, q_ref, o_ref, do_ref, ln_ref, kv_ref,
    dq_ref, part_ref, inverse, terms,
):
    blocks, docs = order_ref.shape[0], lengths_ref.shape[0]
    me = lax.axis_index("ctx")
    scale = 1.0 / math.sqrt(HEAD_SIZE)
    for b in range(blocks):
        inverse[order_ref[b]] = b
    norms = ln_ref[...].reshape(GROUP, 2 * BLOCK).T
    keys_in = window * BLOCK
    nt = (((1,), (1,)), ((), ()))
    tn = (((0,), (0,)), ((), ()))

    def stacked(ref, first):
        return jnp.concatenate(
            [
                ref[first:first + BLOCK, h * HEAD_SIZE:(h + 1) * HEAD_SIZE]
                for h in range(GROUP)
            ],
            axis=0,
        )

    bases = []
    for i in range(2):
        first = i * BLOCK
        at = order_ref[2 * me + i]
        base = at - (window - 1)
        bases.append(base)
        query_pos = at * BLOCK + lax.broadcasted_iota(jnp.int32, (BLOCK, 1), 0)
        start = jnp.zeros((BLOCK, 1), jnp.int32)
        end = jnp.int32(0)
        for d in range(docs):
            end = end + lengths_ref[d]
            start = jnp.where(query_pos >= end, end, start)
        key_pos = base * BLOCK + lax.broadcasted_iota(jnp.int32, (BLOCK, keys_in), 1)
        allowed = ((key_pos >= start) & (key_pos <= query_pos)).astype(F32)
        allowed = jnp.concatenate([allowed] * GROUP, axis=0) > 0.0

        where = [inverse[jnp.maximum(base + w, 0)] for w in range(window)]
        k = jnp.concatenate([kv_ref[b // 2, 0, b % 2] for b in where], axis=0)
        v = jnp.concatenate([kv_ref[b // 2, 1, b % 2] for b in where], axis=0)
        q, o, do = stacked(q_ref, first), stacked(o_ref, first), stacked(do_ref, first)
        dots = jnp.sum(do.astype(F32) * o.astype(F32), axis=1, keepdims=True)
        norm = jnp.concatenate(
            [norms[first:first + BLOCK, h:h + 1] for h in range(GROUP)], axis=0
        )
        scores = lax.dot_general(q, k, nt, preferred_element_type=F32) * scale
        weights = jnp.where(allowed, jnp.exp(scores - norm), 0.0)
        grad_weights = lax.dot_general(do, v, nt, preferred_element_type=F32)
        grad_scores = (weights * (grad_weights - dots) * scale).astype(BF16)
        weights = weights.astype(BF16)
        dq = jnp.dot(grad_scores, k, preferred_element_type=F32).astype(BF16)
        for h in range(GROUP):
            dq_ref[first:first + BLOCK, h * HEAD_SIZE:(h + 1) * HEAD_SIZE] = dq[
                h * BLOCK:(h + 1) * BLOCK
            ]
        dk = lax.dot_general(grad_scores, q, tn, preferred_element_type=F32)
        dv = lax.dot_general(weights, do, tn, preferred_element_type=F32)
        terms[0, i, :window] = dk.reshape(window, BLOCK, HEAD_SIZE)
        terms[1, i, :window] = dv.reshape(window, BLOCK, HEAD_SIZE)
        for kind in range(2):
            terms[kind, i, window] = jnp.zeros((BLOCK, HEAD_SIZE), F32)

    for b in range(blocks):
        slots = []
        for base in bases:
            w = order_ref[b] - base
            slots.append(jnp.where((w >= 0) & (w < window), w, window))
        for kind in range(2):
            part_ref[b // 2, kind, b % 2] = (
                terms[kind, 0, slots[0]] + terms[kind, 1, slots[1]]
            ).astype(BF16)


def terms_of(n, queries, attn_out, grad_out, log_norm, all_kv, doc_lengths, block_order):
    rows, row_width = queries.shape
    local_kv = row_width // (GROUP * HEAD_SIZE)
    blocks = block_order.shape[0]
    window = blocks // 4 + 1
    heads = pl.BlockSpec((rows, GROUP * HEAD_SIZE), lambda g: (0, g))
    pair = pl.BlockSpec((n, 2, 2, BLOCK, HEAD_SIZE), lambda g: (0, 0, 0, 0, g))
    smem = pl.BlockSpec(memory_space=pltpu.SMEM)
    return pl.pallas_call(
        functools.partial(terms_kernel, window),
        grid=(local_kv,),
        out_shape=[
            jax.ShapeDtypeStruct((rows, row_width), BF16),
            jax.ShapeDtypeStruct(all_kv.shape, BF16),
        ],
        in_specs=[
            smem, smem, heads, heads, heads,
            pl.BlockSpec((GROUP, rows), lambda g: (g, 0)),
            pair,
        ],
        out_specs=[heads, pair],
        scratch_shapes=[
            pltpu.SMEM((blocks,), jnp.int32),
            pltpu.VMEM((2, 2, window + 1, BLOCK, HEAD_SIZE), F32),
        ],
        compiler_params=pltpu.CompilerParams(vmem_limit_bytes=VMEM_LIMIT),
        name="attention_terms",
    )(block_order, doc_lengths, queries, attn_out, grad_out, log_norm, all_kv)


def on_device(queries, keys, values, attn_out, grad_out, log_norm, doc_lengths, block_order):
    n = lax.axis_size("ctx")
    rows, width = keys.shape
    all_kv = gather(n, keys, values).reshape(n, 2, 2, BLOCK, width)
    grad_q, parts = terms_of(
        n, queries, attn_out, grad_out, log_norm, all_kv, doc_lengths, block_order
    )
    grad_k, grad_v = reduce_to_owner(n, parts.reshape(n, 2, rows, width))
    return (grad_q, grad_k, grad_v)


def solution(mesh):
    whole = P(("dp", "ctx"), "tensor")
    return jax.shard_map(
        on_device,
        mesh=mesh,
        in_specs=(whole,) * 5 + (P("tensor", ("dp", "ctx")), P("dp"), P("dp")),
        out_specs=(whole,) * 3,
        check_vma=False,
    )
```

time: 197 us -> 72.4 us (0.37)
  waiting for transfers between devices: 84.7 us -> 0 us
  Pallas kernels: 0 us -> 65.7 us
  local copies, waits for them, and re-layouts: 42.2 us -> 5.77 us
  other arithmetic: 32.4 us -> 0 us
  matrix products: 20.7 us -> 0 us
  starting transfers between devices: 14.4 us -> 0 us
    all_to_all x1 -> x0, waiting for transfers between devices: 81.9 us -> none  [on_device(): lax.all_to_all(stored, 'ctx', split_axis=0, concat_axis=0, tiled=True)]
    pallas_call x0 -> x3, Pallas kernels: none -> 65.7 us  [the longest x1 28 us: gather(): pl.pallas_call(functools.partial(gather_kernel, n), out_shape=jax.ShapeDt...]
    dot_general x40 -> x0, matrix products: 20.7 us -> none  [the longest x8 4.8 us: full_terms(): jnp.einsum('rkgd,ckd->kgrc', query_heads, key_block, preferred_element_ty...]
    while x36 -> x0, local copies, waits for them, and re-layouts: 19.8 us -> none
    add x15 -> x0, other arithmetic: 14.4 us -> none  [the longest x8 11.6 us: positions(): position = starts + local_rows % half_rows]
    ppermute x7 -> x0, starting transfers between devices: 9.6 us -> none  [from_behind(): return lax.ppermute(block, axis, route)]
    dynamic_update_slice x8 -> x0, other arithmetic: 6.74 us -> none  [absorb(): return lax.dynamic_update_index_in_dim(stored, partial_value, source, 0)]
    all_to_all x1 -> x0, starting transfers between devices: 4.78 us -> none  [on_device(): lax.all_to_all(stored, 'ctx', split_axis=0, concat_axis=0, tiled=True)]
  transfers between devices with their start and end apart: 8 -> 0, of which waited for: 4 -> 0; matrix products, arithmetic and copies ran while one was open for 25% -> 0% of each run, Pallas kernels for 0% -> 0%
where the time goes in v1:
time: 72.4 us; the launch traced here: 72.2 us
  Pallas kernels  65.7 us (91%)
  local copies, waits for them, and re-layouts  5.77 us (8%)
    pallas_call x1, Pallas kernels, gather(): pl.pallas_call(functools.partial(gather_kernel, n), out_shape=jax.ShapeDt...  28 us
    pallas_call x1, Pallas kernels, reduce_to_owner(): pl.pallas_call(functools.partial(reduce_kernel, n), out_shape=[jax.ShapeD...  24.6 us
    pallas_call x1, Pallas kernels, terms_of(): pl.pallas_call(functools.partial(terms_kernel, window), grid=(local_kv,),...  13.1 us
    unnamed x20, local copies, waits for them, and re-layouts  5.77 us

profile of v1, /device:TPU:0, one launch (start us, length us, event | category | flops | bytes accessed | tf_op | source)
XLA Modules:
  0.0 72.2 jit_solution(10136817167190917418)
XLA Ops:
  0.6 0.0 copy-start.2
  0.6 0.0 copy-start.4
  0.7 1.0 %copy-done.4 = bf16[128,512]{1,0:T(8,128)(2,1)S(1)} copy-done((bf16[128,512]{1,0:T(8,128)(2,1)S(1)}, bf16[128,512]{1,0:T(8,128)(2,1)}, u32[]{:S(2)}) %copy-start.4) | copy-done | bytes 131096
  1.6 0.0 copy-start.5
  1.6 0.9 %copy-done.5 = bf16[128,512]{1,0:T(8,128)(2,1)S(1)} copy-done((bf16[128,512]{1,0:T(8,128)(2,1)S(1)}, bf16[128,512]{1,0:T(8,128)(2,1)}, u32[]{:S(2)}) %copy-start.5) | copy-done | bytes 131096
  2.5 0.0 copy-start.1
  2.5 0.0 copy-start.6
  2.5 0.0 copy-start.7
  2.5 0.0 copy-start.8
  2.6 28.0 %gather_kv.1 = bf16[8,2,128,512]{3,2,1,0:T(8,128)(2,1)S(1)} custom-call(bf16[128,512]{1,0:T(8,128)(2,1)S(1)} %copy-done.4, bf16[128,512]{1,0:T(8,128)(2,1)S(1)} %copy-done.5), custom_call_target="tpu_custom_call" | custom-call | tf_op jit(solution)/shard_map/gather_kv/pallas_call | solution.py:139
  30.6 0.0 copy-start
  30.6 1.3 %copy-done = bf16[8,2,128,512]{3,2,1,0:T(8,128)(2,1)} copy-done((bf16[8,2,128,512]{3,2,1,0:T(8,128)(2,1)}, bf16[8,2,128,512]{3,2,1,0:T(8,128)(2,1)S(1)}, u32[]{:S(2)}) %copy-start) | copy-done | bytes 2097176
  31.9 0.0 copy-done.2
  31.9 0.0 copy-done.1
  31.9 0.0 copy-done.6
  31.9 0.0 copy-done.7
  31.9 0.0 copy-done.8
  31.9 0.0 copy-start.3
  32.0 1.2 %copy-done.3 = bf16[128,4096]{1,0:T(8,128)(2,1)S(1)} copy-done((bf16[128,4096]{1,0:T(8,128)(2,1)S(1)}, bf16[128,4096]{1,0:T(8,128)(2,1)}, u32[]{:S(2)}) %copy-start.3) | copy-done | bytes 1048600
  33.2 13.1 %attention_terms.1 = (bf16[128,4096]{1,0:T(8,128)(2,1)}, bf16[8,2,2,64,512]{4,3,2,1,0:T(8,128)(2,1)S(1)}) custom-call(s32[16]{0:T(128)S(1)} %copy-done.7, s32[16]{0:T(128)S(1)} %copy-done.8, bf16[128,4096]{1,0:T(8,128)(2,1)S(1)} %copy-done.1, bf16[128,4096]{1,0:T(8,128)(2,1)S(1)} %copy-done.2, bf16[128,4096]{1,0:T(8,128)(2,1)S(1)} %copy-done.3, ...), custom_call_target="tpu_custom_call" | custom-call | tf_op jit(solution)/shard_map/attention_terms/pallas_call | solution.py:362
  46.3 24.6 %reduce_kv_grads.1 = (bf16[128,512]{1,0:T(8,128)(2,1)S(1)}, bf16[128,512]{1,0:T(8,128)(2,1)S(1)}) custom-call(bf16[8,2,128,512]{3,2,1,0:T(8,128)(2,1)S(1)} %bitcast.3), custom_call_target="tpu_custom_call" | custom-call | tf_op jit(solution)/shard_map/reduce_kv_grads/pallas_call | solution.py:266
  70.8 0.7 copy.13
  71.5 0.7 copy.14
Async XLA Ops:
  0.6 31.3 %copy-start.2 = (bf16[128,4096]{1,0:T(8,128)(2,1)S(1)}, bf16[128,4096]{1,0:T(8,128)(2,1)}, u32[]{:S(2)}) copy-start(bf16[128,4096]{1,0:T(8,128)(2,1)} %o_ref.1) | copy-start | bytes 3145732
  0.6 1.0 %copy-start.4 = (bf16[128,512]{1,0:T(8,128)(2,1)S(1)}, bf16[128,512]{1,0:T(8,128)(2,1)}, u32[]{:S(2)}) copy-start(bf16[128,512]{1,0:T(8,128)(2,1)} %k_ref.1) | copy-start | bytes 393220
  1.6 0.9 %copy-start.5 = (bf16[128,512]{1,0:T(8,128)(2,1)S(1)}, bf16[128,512]{1,0:T(8,128)(2,1)}, u32[]{:S(2)}) copy-start(bf16[128,512]{1,0:T(8,128)(2,1)} %v_ref.1) | copy-start | bytes 393220
  2.5 29.4 %copy-start.1 = (bf16[128,4096]{1,0:T(8,128)(2,1)S(1)}, bf16[128,4096]{1,0:T(8,128)(2,1)}, u32[]{:S(2)}) copy-start(bf16[128,4096]{1,0:T(8,128)(2,1)} %q_ref.1) | copy-start | bytes 3145732
  2.5 29.4 %copy-start.6 = (f32[32,128]{1,0:T(8,128)S(1)}, f32[32,128]{1,0:T(8,128)}, u32[]{:S(2)}) copy-start(f32[32,128]{1,0:T(8,128)} %ln_ref.1) | copy-start | bytes 49156
  2.5 29.4 %copy-start.7 = (s32[16]{0:T(128)S(1)}, s32[16]{0:T(128)}, u32[]{:S(2)}) copy-start(s32[16]{0:T(128)} %order_ref.1) | copy-start | bytes 196
  2.5 29.4 %copy-start.8 = (s32[16]{0:T(128)S(1)}, s32[16]{0:T(128)}, u32[]{:S(2)}) copy-start(s32[16]{0:T(128)} %lengths_ref.1) | copy-start | bytes 196
  30.6 1.3 %copy-start = (bf16[8,2,128,512]{3,2,1,0:T(8,128)(2,1)}, bf16[8,2,128,512]{3,2,1,0:T(8,128)(2,1)S(1)}, u32[]{:S(2)}) copy-start(bf16[8,2,128,512]{3,2,1,0:T(8,128)(2,1)S(1)} %gather_kv.1) | copy-start | bytes 6291460
  31.9 1.2 %copy-start.3 = (bf16[128,4096]{1,0:T(8,128)(2,1)S(1)}, bf16[128,4096]{1,0:T(8,128)(2,1)}, u32[]{:S(2)}) copy-start(bf16[128,4096]{1,0:T(8,128)(2,1)} %do_ref.1) | copy-start | bytes 3145732
